TPU v7x, 32 devices: a whole 2x2x4 slice. The times are simulated.
32 devices in a mesh: sub: 8 (over z, y), grp: 4 (over x, core).
Axes of the slice: x: 2, y: 2, z: 4, core: 2. Of those that a mesh axis runs over, the one named last changes fastest.
Arguments:
- facies: int32 [128, 32, 128], P('sub', 'grp'), may hold values from 0 to 7
- facies_perm: float32 [8], replicated, may hold values from 0.2 to 5
- perm_scale: float32 [128, 32, 128], P('sub', 'grp'), may hold values from 0.5 to 2
- source: float32 [128, 32, 128], P('sub', 'grp'), may hold values from -6 to 6
- pressure_start: float32 [128, 32, 128], P('sub', 'grp'), may hold values from -4 to 4
- intersection_depth: int32 [7], replicated, may hold values from 1 to 4, as said below
Outputs:
- pressure: float32 [128, 32, 128], P('sub', 'grp')
Inputs may be any that keep to these rules, and one draw needn't show every extreme that they name: `intersection_depth`: every entry is a margin depth; some entry equals 4 in every draw.
All inputs are finite; a program needn't handle non-finite values.
Results may differ from a plain program's by a relative error of at most 0.0003.
Values sent between devices are 32-bit elements; how exact they have to be, the bound alone decides.
A program may use at most 64 MiB of HBM per device.

v0:
```python
import functools
import math

import jax
import jax.numpy as jnp
from jax import lax
from jax.experimental import pallas as pl
from jax.experimental.pallas import tpu as pltpu
from jax.sharding import PartitionSpec as P

OV = 4
BL = 8
ROUNDS = 4
OUTER = 2
FACIES = 8
STORE = 0.02
MESH = pl.DeviceIdType.MESH

OWN = 16
ROWS = OWN + 2 * OV
WIDE = ROWS + 2
LANES = 128
CHUNKS = ROWS // BL
CH = BL * 8

DIRS = ((-1, 0), (1, 0), (0, -1), (0, 1), (-1, -1), (-1, 1), (1, -1), (1, 1))
OPP = tuple(DIRS.index((-a, -b)) for a, b in DIRS)


def relax_weight(k):
    return 1.0 / (1.4 + 0.6 * math.cos(math.pi * (2 * k + 1) / (2 * ROUNDS)))


def harmonic(a, b):
    return 2.0 * a * b / jnp.maximum(a + b, 1e-30)


def roll_x(v, s):
    return pltpu.roll(v.reshape(v.shape[0] // 8, 8, LANES), s % 8, 1).reshape(v.shape)


def roll_y(v, s):
    return pltpu.roll(v, s % LANES, 1)


def roll_z(v, s):
    return pltpu.roll(v, s % v.shape[0], 0)


def reduce_factors(low, high, roll):
    l, u, d = -low, -high, None
    parts = []
    for s in (1, 2, 4):
        if d is None:
            a, b, d = low, high, jnp.ones_like(low)
        else:
            rd = 1.0 / d
            a, b = -l * roll(rd, s), -u * roll(rd, -s)
        d = d + a * roll(u, s) + b * roll(l, -s)
        l, u = a * roll(l, s), b * roll(u, -s)
        parts += [a, b]
    return parts + [1.0 / d]


def reduce_x(r, f):
    a1, b1, a2, b2, c3, iv = f
    r = r + a1 * roll_x(r, 1) + b1 * roll_x(r, -1)
    r = r + a2 * roll_x(r, 2) + b2 * roll_x(r, -2)
    r = r + c3 * roll_x(r, 4)
    return r * iv


def reduce_y(r, f):
    a1, b1, a2, b2, a3, b3, iv = f
    r = r + a1 * roll_y(r, 1) + b1 * roll_y(r, -1)
    r = r + a2 * roll_y(r, 2) + b2 * roll_y(r, -2)
    r = r + a3 * roll_y(r, 4) + b3 * roll_y(r, -4)
    return r * iv


def col(x, planes=ROWS, first=0):
    return pl.ds(first * 8 + x, planes, stride=8)


def kernel(
    fac, fperm, pscale, src, p0, depth, out,
    zs, xs, ds, zr, xr, dr, mx, mzr, mxr, mdr, fzr, cs, cr,
    perm, pres, sper, spre, isrc, tgt, tside, e0, e1, e2, ub, corr,
    co, xf, yf, zf, gx, cx, sco, syf,
    i_send, i_recv, m_send, m_recv, f_send, f_recv, c_send, c_recv,
):
    n_sub, n_grp = lax.axis_size("sub"), lax.axis_size("grp")
    sub, grp = lax.axis_index("sub"), lax.axis_index("grp")
    has_axis = {
        (-1, 0): sub > 0,
        (1, 0): sub < n_sub - 1,
        (0, -1): grp > 0,
        (0, 1): grp < n_grp - 1,
    }
    has = []
    for dz, dx in DIRS:
        if dz and dx:
            has.append(jnp.logical_and(has_axis[(dz, 0)], has_axis[(0, dx)]))
        else:
            has.append(has_axis[(dz, dx)])

    def peer(d):
        return {"sub": sub + DIRS[d][0], "grp": grp + DIRS[d][1]}

    def remote(d, a, b, s_sem, r_sem):
        return pltpu.make_async_remote_copy(
            src_ref=a, dst_ref=b, send_sem=s_sem, recv_sem=r_sem,
            device_id=peer(d), device_id_type=MESH,
        )

    def exchange_start(dirs, make):
        for d in dirs:
            @pl.when(has[d])
            def _(d=d):
                make(d, OPP[d]).start()

    def exchange_wait(dirs, make):
        for d in dirs:
            @pl.when(has[d])
            def _(d=d):
                make(d, OPP[d]).wait_send()
                make(d, d).wait_recv()

    for d in range(8):
        @pl.when(jnp.logical_not(has[d]))
        def _(d=d):
            if d < 2:
                zr[d] = jnp.zeros(zr.shape[1:], jnp.float32)
                mzr[d] = jnp.zeros(mzr.shape[1:], jnp.float32)
                fzr[d] = jnp.zeros(fzr.shape[1:], jnp.float32)
            elif d < 4:
                xr[d - 2] = jnp.zeros(xr.shape[1:], jnp.float32)
                mxr[d - 2] = jnp.zeros(mxr.shape[1:], jnp.float32)
                for ph in range(cr.shape[0]):
                    cr[ph, d - 2] = jnp.zeros(cr.shape[2:], jnp.float32)
            else:
                dr[d - 4] = jnp.zeros(dr.shape[1:], jnp.float32)
                mdr[d - 4] = jnp.zeros(mdr.shape[1:], jnp.float32)

    barrier = pltpu.get_barrier_semaphore()
    for d in range(8):
        @pl.when(has[d])
        def _(d=d):
            pl.semaphore_signal(barrier, inc=1, device_id=peer(d), device_id_type=MESH)

    kinds = fac[...]
    own = jnp.zeros(kinds.shape, jnp.float32)
    for kind in range(FACIES):
        own = jnp.where(kinds == kind, fperm[kind], own)
    own = (own * pscale[...]).reshape(OWN * 8, LANES)
    perm[pl.ds(40, OWN * 8)] = own
    pres[pl.ds(40, OWN * 8)] = p0[...].reshape(OWN * 8, LANES)
    isrc[pl.ds(32, OWN * 8)] = src[...].reshape(OWN * 8, LANES)
    for s in range(2):
        at = 5 if s == 0 else 16
        zs[s, pl.ds(0, 40)] = perm[pl.ds(at * 8, 40)]
        zs[s, pl.ds(40, 40)] = pres[pl.ds(at * 8, 40)]
        zs[s, pl.ds(80, 32)] = isrc[pl.ds(32 if s == 0 else 128, 32)]
        near, far = (0, 1) if s == 0 else (7, 6)
        kn, kf, pn = perm[col(near, 16, 5)], perm[col(far, 16, 5)], pres[col(near, 16, 5)]
        xs[s, pl.ds(0, 16)] = kn
        xs[s, pl.ds(16, 16)] = kf
        xs[s, pl.ds(32, 16)] = pn
        for z in range(2):
            at_rows = 5 if z == 0 else 13
            ds[2 * z + s, pl.ds(0, 8)] = perm[col(near, 8, at_rows)]
            ds[2 * z + s, pl.ds(8, 8)] = perm[col(far, 8, at_rows)]
            ds[2 * z + s, pl.ds(16, 8)] = pres[col(near, 8, at_rows)]

    def init_copy(d, slot):
        if d < 2:
            a, b = zs.at[d], zr.at[slot]
        elif d < 4:
            a, b = xs.at[d - 2], xr.at[slot - 2]
        else:
            a, b = ds.at[d - 4], dr.at[slot - 4]
        return remote(d, a, b, i_send.at[d], i_recv.at[slot])

    pl.semaphore_wait(barrier, sum(jnp.where(h, 1, 0) for h in has))
    exchange_start(range(8), init_copy)

    low = jnp.where(sub > 0, depth[jnp.maximum(sub - 1, 0)], 0)
    high = jnp.where(sub < n_sub - 1, depth[jnp.minimum(sub, n_sub - 2)], 0)

    def active(rows):
        inside = (rows >= OV - low) & (rows < OV + OWN + high)
        return jnp.where(inside, 1.0, 0.0)

    def rows_of(c):
        return lax.broadcasted_iota(jnp.int32, (8, 8, LANES), 0).reshape(CH, LANES) + 8 * c

    lane = lax.broadcasted_iota(jnp.int32, (CH, LANES), 1)
    lane2 = lax.broadcasted_iota(jnp.int32, (ROWS, LANES), 1)
    row2 = lax.broadcasted_iota(jnp.int32, (ROWS, LANES), 0)
    subl = lax.broadcasted_iota(jnp.int32, (8, 8, LANES), 1).reshape(CH, LANES)
    zeros_plane = jnp.zeros((8, LANES), jnp.float32)
    for e in (e0, e1, e2):
        e[pl.ds(0, 8)] = zeros_plane
        e[pl.ds((ROWS + 1) * 8, 8)] = zeros_plane

    exchange_wait(range(8), init_copy)

    perm[pl.ds(0, 40)] = zr[0, pl.ds(0, 40)]
    pres[pl.ds(0, 40)] = zr[0, pl.ds(40, 40)]
    isrc[pl.ds(0, 32)] = zr[0, pl.ds(80, 32)]
    perm[pl.ds(168, 40)] = zr[1, pl.ds(0, 40)]
    pres[pl.ds(168, 40)] = zr[1, pl.ds(40, 40)]
    isrc[pl.ds(160, 32)] = zr[1, pl.ds(80, 32)]
    for s in range(2):
        for f in range(2):
            sper[s, f, pl.ds(5, 16)] = xr[s, pl.ds(16 * f, 16)]
            sper[s, f, pl.ds(0, 5)] = dr[s, pl.ds(8 * f + 3, 5)]
            sper[s, f, pl.ds(21, 5)] = dr[2 + s, pl.ds(8 * f, 5)]
        spre[s, pl.ds(4, 16)] = xr[s, pl.ds(32, 16)]
        spre[s, pl.ds(0, 4)] = dr[s, pl.ds(20, 4)]
        spre[s, pl.ds(20, 4)] = dr[2 + s, pl.ds(16, 4)]
        ub[col(7 * s)] = sper[s, 0, pl.ds(1, ROWS)]

    for c in range(CHUNKS):
        here = pl.ds(c * CH, CH)
        mid = perm[pl.ds((c * 8 + 1) * 8, CH)]
        edge = ub[here]
        fb = harmonic(perm[pl.ds(c * CH, CH)], mid)
        fa = harmonic(mid, perm[pl.ds((c * 8 + 2) * 8, CH)])
        fl = harmonic(jnp.where(subl == 0, edge, roll_x(mid, 1)), mid)
        fr = harmonic(mid, jnp.where(subl == 7, edge, roll_x(mid, -1)))
        ff = harmonic(jnp.where(lane == 0, 0.0, roll_y(mid, 1)), mid)
        fk = harmonic(mid, jnp.where(lane == LANES - 1, 0.0, roll_y(mid, -1)))
        act = active(rows_of(c))
        inv = act / (STORE + fb + fa + fl + fr + ff + fk)
        fl, fr = fl * inv, fr * inv
        ub[here] = jnp.where(subl == 0, fl, fr)
        fl, fr = jnp.where(subl == 0, 0.0, fl), jnp.where(subl == 7, 0.0, fr)
        fb, fa, ff, fk = fb * inv, fa * inv, ff * inv, fk * inv
        for i, f in enumerate((fb, fa, fl, fr, ff, fk)):
            co[i, here] = f
        isrc[here] = isrc[here] * inv
        a1, b1, a2, b2, a3, b3, iv = reduce_factors(fl, fr, roll_x)
        for i, f in enumerate((a2, b2, a3 + b3, iv)):
            xf[i, here] = f
        fy = reduce_factors(
            jnp.where(lane % BL == 0, 0.0, ff), jnp.where(lane % BL == BL - 1, 0.0, fk), roll_y
        )
        for i, f in enumerate(fy):
            yf[i, here] = f
        lz = -fb * active(rows_of(c) - 1)
        uz = -fa * active(rows_of(c) + 1)
        d = None
        for i in range(BL):
            at = pl.ds(c * CH + i * 8, 8)
            part = slice(i * 8, i * 8 + 8)
            if i == 0:
                m, d = zeros_plane, jnp.ones((8, LANES), jnp.float32)
            else:
                m = lz[part] / d
                d = 1.0 - m * uz[(i - 1) * 8 : i * 8]
            zf[0, at] = m
            zf[1, at] = 1.0 / d
            zf[2, at] = uz[part] / d
    for s in range(2):
        cx[s] = ub[col(7 * s)]

    def xfac(here):
        return [co[2, here], co[3, here]] + [xf[i, here] for i in range(4)]

    for c in range(CHUNKS):
        here = pl.ds(c * CH, CH)
        edge, f = ub[here], xfac(here)
        for s in range(2):
            gx[s, here] = reduce_x(jnp.where(subl == 7 * s, edge, 0.0), f)

    for s in range(2):
        mid = sper[s, 0, pl.ds(1, ROWS)]
        fb = harmonic(sper[s, 0, pl.ds(0, ROWS)], mid)
        fa = harmonic(mid, sper[s, 0, pl.ds(2, ROWS)])
        fx = harmonic(mid, sper[s, 1, pl.ds(1, ROWS)])
        fo = harmonic(mid, perm[col(7 * s, ROWS, 1)])
        ff = harmonic(jnp.where(lane2 == 0, 0.0, roll_y(mid, 1)), mid)
        fk = harmonic(mid, jnp.where(lane2 == LANES - 1, 0.0, roll_y(mid, -1)))
        inv = active(row2) / (STORE + fb + fa + fx + fo + ff + fk)
        fb = jnp.where(row2 == 0, 0.0, fb * inv)
        fa = jnp.where(row2 == ROWS - 1, 0.0, fa * inv)
        ff, fk = ff * inv, fk * inv
        for i, f in enumerate((fb, fa, fx * inv, fo * inv, ff, fk)):
            sco[s, i] = f
        fy = reduce_factors(
            jnp.where(lane2 % BL == 0, 0.0, ff), jnp.where(lane2 % BL == BL - 1, 0.0, fk), roll_y
        )
        for i, f in enumerate(fy):
            syf[s, i] = f

    def update(t, e, c, scale=None):
        here = pl.ds(c * CH, CH)
        v = e[pl.ds((c * 8 + 1) * 8, CH)]
        u = t[here] - (v if scale is None else v * scale)
        u = u + co[0, here] * e[pl.ds(c * CH, CH)] + co[1, here] * e[pl.ds((c * 8 + 2) * 8, CH)]
        u = u + co[2, here] * roll_x(v, 1) + co[3, here] * roll_x(v, -1)
        return v, u + co[4, here] * roll_y(v, 1) + co[5, here] * roll_y(v, -1)

    def col_copy(ph, rows):
        def make(d, slot):
            return remote(
                d, cs.at[ph, d - 2, pl.ds(0, rows)], cr.at[ph, slot - 2, pl.ds(0, rows)],
                c_send.at[ph, d - 2], c_recv.at[ph, slot - 2],
            )
        return make

    def one_round(outer, k):
        first = isinstance(k, int)
        ph = outer * 2 * ROUNDS + 2 * k
        om = relax_weight(0)
        if not first:
            for i in range(1, ROUNDS):
                om = jnp.where(k == i, jnp.float32(relax_weight(i)), om)
        for c in range(CHUNKS):
            here = pl.ds(c * CH, CH)
            if first:
                e1[pl.ds((c * 8 + 1) * 8, CH)] = om * reduce_x(tgt[here], xfac(here))
            else:
                v, u = update(tgt, e0, c)
                e1[pl.ds((c * 8 + 1) * 8, CH)] = v + om * reduce_x(u, xfac(here))
        if not first:
            exchange_wait((2, 3), col_copy(ph, ROWS))
            for z in range(ROWS):
                at, here = pl.ds((z + 1) * 8, 8), pl.ds(z * 8, 8)
                left = jnp.broadcast_to(cr[ph, 0, pl.ds(z, 1)], (8, LANES))
                right = jnp.broadcast_to(cr[ph, 1, pl.ds(z, 1)], (8, LANES))
                e1[at] = e1[at] + om * (gx[0, here] * left + gx[1, here] * right)
        ph = ph + 1
        for s in range(2):
            near, far = (0, 1) if s == 0 else (7, 6)
            cs[ph, s, pl.ds(0, ROWS)] = e1[col(near, ROWS, 1)]
            cs[ph, s, pl.ds(ROWS, ROWS)] = e1[col(far, ROWS, 1)]
            if first:
                cs[ph, s, pl.ds(2 * ROWS, ROWS)] = tgt[col(near)]
        make = col_copy(ph, (3 if first else 2) * ROWS)
        exchange_start((2, 3), make)
        for c in range(CHUNKS):
            here = pl.ds(c * CH, CH)
            v, u = update(tgt, e1, c)
            e2[pl.ds((c * 8 + 1) * 8, CH)] = v + om * reduce_y(u, [yf[i, here] for i in range(7)])
        exchange_wait((2, 3), make)
        beside = []
        for s in range(2):
            near, far = cr[ph, s, pl.ds(0, ROWS)], cr[ph, s, pl.ds(ROWS, ROWS)]
            if first:
                tside[s] = cr[ph, s, pl.ds(2 * ROWS, ROWS)]
            inner = e1[col(7 * s, ROWS, 1)]
            u = tside[s] - near
            u = u + sco[s, 0] * roll_z(near, 1) + sco[s, 1] * roll_z(near, -1)
            u = u + sco[s, 2] * far + sco[s, 3] * inner
            u = u + sco[s, 4] * roll_y(near, 1) + sco[s, 5] * roll_y(near, -1)
            beside.append(near + om * reduce_y(u, [syf[s, i] for i in range(7)]))
            f = [yf[i, col(7 * s)] for i in range(7)]
            at = col(7 * s, ROWS, 1)
            e2[at] = e2[at] + om * reduce_y(cx[s] * near, f)
        for c in range(CHUNKS):
            ub[pl.ds(c * CH, CH)] = update(tgt, e2, c)[1]
        for s in range(2):
            at = col(7 * s)
            ub[at] = ub[at] + cx[s] * beside[s]
        for c in range(CHUNKS):
            fw, prev = [], None
            for i in range(BL):
                at = pl.ds(c * CH + i * 8, 8)
                prev = ub[at] if i == 0 else ub[at] - zf[0, at] * prev
                fw.append(prev)
            nxt = None
            for i in range(BL - 1, -1, -1):
                at = pl.ds(c * CH + i * 8, 8)
                nxt = fw[i] * zf[1, at] if nxt is None else fw[i] * zf[1, at] - zf[2, at] * nxt
                to = pl.ds((c * 8 + i + 1) * 8, 8)
                e0[to] = e2[to] + om * nxt

        def send_next():
            for s in range(2):
                cs[ph + 1, s, pl.ds(0, ROWS)] = e0[col(7 * s, ROWS, 1)]
            exchange_start((2, 3), col_copy(ph + 1, ROWS))

        if first:
            send_next()
        else:
            pl.when(k < ROUNDS - 1)(send_next)

    def mid_copy(d, slot):
        if d < 2:
            a, b = corr.at[pl.ds(0 if d == 0 else 120, 72)], mzr.at[slot]
        elif d < 4:
            a, b = mx.at[d - 2], mxr.at[slot - 2]
        else:
            z, s = divmod(d - 4, 2)
            a, b = mx.at[s, pl.ds(16 * z, 8)], mdr.at[slot - 4]
        return remote(d, a, b, m_send.at[d], m_recv.at[slot])

    def end_copy(d, slot):
        a = corr.at[pl.ds(0 if d == 0 else 160, 32)]
        return remote(d, a, fzr.at[slot], f_send.at[d], f_recv.at[slot])

    for outer in range(OUTER):
        for c in range(CHUNKS):
            tgt[pl.ds(c * CH, CH)] = update(isrc, pres, c, active(rows_of(c)))[1]
        for s in range(2):
            tgt[col(7 * s)] = tgt[col(7 * s)] + cx[s] * spre[s]
        one_round(outer, 0)

        def step(k, carry, outer=outer):
            one_round(outer, k)
            return carry

        lax.fori_loop(1, ROUNDS, step, 0)
        for c in range(CHUNKS):
            rows = rows_of(c)
            band = (rows < OV + low) | (rows >= OV + OWN - high)
            w = active(rows) * jnp.where(band, 0.5, 1.0)
            corr[pl.ds(c * CH, CH)] = w * e0[pl.ds((c * 8 + 1) * 8, CH)]
        if outer == 0:
            for s in range(2):
                mx[s] = corr[col(7 * s)]
            exchange_start(range(8), mid_copy)
            pres[pl.ds(8, ROWS * 8)] = pres[pl.ds(8, ROWS * 8)] + corr[...]
            exchange_wait(range(8), mid_copy)
            for z in range(2):
                at = pl.ds(0 if z == 0 else 17 * 8, 72)
                pres[at] = pres[at] + mzr[z]
            for s in range(2):
                spre[s] = spre[s] + mxr[s]
                for z in range(2):
                    at = pl.ds(16 * z, 8)
                    spre[s, at] = spre[s, at] + mdr[2 * z + s]
        else:
            exchange_start((0, 1), end_copy)
            pres[pl.ds(8, ROWS * 8)] = pres[pl.ds(8, ROWS * 8)] + corr[...]
            exchange_wait((0, 1), end_copy)
            for z in range(2):
                at = pl.ds(40 if z == 0 else 17 * 8, 32)
                pres[at] = pres[at] + fzr[z]
    out[...] = pres[pl.ds(40, OWN * 8)].reshape(OWN, 8, LANES)


def on_device(facies, facies_perm, perm_scale, source, pressure_start, intersection_depth):
    assert source.shape == (OWN, 8, LANES)
    f32 = jnp.float32

    def buf(*shape):
        return pltpu.VMEM(shape, f32)

    field, wide = (ROWS * 8, LANES), (WIDE * 8, LANES)
    phases = OUTER * 2 * ROUNDS
    scratch = [
        buf(2, 112, LANES), buf(2, 48, LANES), buf(4, 24, LANES),
        buf(2, 112, LANES), buf(2, 48, LANES), buf(4, 24, LANES),
        buf(2, ROWS, LANES), buf(2, 72, LANES), buf(2, ROWS, LANES), buf(4, 8, LANES),
        buf(2, 32, LANES), buf(phases, 2, 3 * ROWS, LANES), buf(phases, 2, 3 * ROWS, LANES),
        buf(*wide), buf(*wide), buf(2, 2, 32, LANES), buf(2, ROWS, LANES),
        buf(*field), buf(*field), buf(2, ROWS, LANES),
        buf(*wide), buf(*wide), buf(*wide), buf(*field), buf(*field),
        buf(6, *field), buf(4, *field), buf(7, *field), buf(3, *field),
        buf(2, *field), buf(2, ROWS, LANES), buf(2, 6, ROWS, LANES), buf(2, 7, ROWS, LANES),
    ]
    sems = [pltpu.SemaphoreType.DMA((n,)) for n in (8, 8, 8, 8, 2, 2)]
    sems += [pltpu.SemaphoreType.DMA((phases, 2)) for _ in range(2)]
    vmem, smem = pl.BlockSpec(memory_space=pltpu.VMEM), pl.BlockSpec(memory_space=pltpu.SMEM)
    return pl.pallas_call(
        kernel,
        out_shape=jax.ShapeDtypeStruct(source.shape, f32),
        in_specs=[vmem, smem, vmem, vmem, vmem, smem],
        out_specs=vmem,
        scratch_shapes=scratch + sems,
        compiler_params=pltpu.CompilerParams(
            collective_id=0, has_side_effects=True, vmem_limit_bytes=32 * 1024 * 1024
        ),
        name="schwarz",
    )(facies, facies_perm, perm_scale, source, pressure_start, intersection_depth)


def solution(mesh):
    return jax.shard_map(
        on_device,
        mesh=mesh,
        in_specs=(
            P("sub", "grp", None),
            P(),
            P("sub", "grp", None),
            P("sub", "grp", None),
            P("sub", "grp", None),
            P(),
        ),
        out_specs=P("sub", "grp", None),
        check_vma=False,
    )
```

profile of v0, /device:TPU:0, one launch (start us, length us, event | category | flops | bytes accessed | tf_op | source)
XLA Modules:
  0.0 59.7 jit_solution(7300161148620258413)
XLA Ops:
  0.0 0.0 copy-start
  0.0 0.8 %copy-done = s32[16,8,128]{2,1,0:T(8,128)S(1)} copy-done((s32[16,8,128]{2,1,0:T(8,128)S(1)}, s32[16,8,128]{2,1,0:T(8,128)}, u32[]{:S(2)}) %copy-start) | copy-done | bytes 65560
  0.8 0.0 copy-start.1
  0.8 0.8 %copy-done.1 = f32[16,8,128]{2,1,0:T(8,128)S(1)} copy-done((f32[16,8,128]{2,1,0:T(8,128)S(1)}, f32[16,8,128]{2,1,0:T(8,128)}, u32[]{:S(2)}) %copy-start.1) | copy-done | bytes 65560
  1.7 0.0 copy-start.2
  1.7 0.8 %copy-done.2 = f32[16,8,128]{2,1,0:T(8,128)S(1)} copy-done((f32[16,8,128]{2,1,0:T(8,128)S(1)}, f32[16,8,128]{2,1,0:T(8,128)}, u32[]{:S(2)}) %copy-start.2) | copy-done | bytes 65560
  2.5 0.0 copy-start.3
  2.5 0.8 %copy-done.3 = f32[16,8,128]{2,1,0:T(8,128)S(1)} copy-done((f32[16,8,128]{2,1,0:T(8,128)S(1)}, f32[16,8,128]{2,1,0:T(8,128)}, u32[]{:S(2)}) %copy-start.3) | copy-done | bytes 65560
  3.4 0.0 copy-start.4
  3.4 0.7 %copy-done.4 = f32[8]{0:T(128)S(1)} copy-done((f32[8]{0:T(128)S(1)}, f32[8]{0:T(128)}, u32[]{:S(2)}) %copy-start.4) | copy-done | bytes 56
  4.0 0.0 copy-start.5
  4.0 0.7 %copy-done.5 = s32[7]{0:T(128)S(1)} copy-done((s32[7]{0:T(128)S(1)}, s32[7]{0:T(128)}, u32[]{:S(2)}) %copy-start.5) | copy-done | bytes 52
  4.7 54.4 %schwarz.1 = f32[16,8,128]{2,1,0:T(8,128)S(1)} custom-call(s32[16,8,128]{2,1,0:T(8,128)S(1)} %copy-done, f32[8]{0:T(128)S(1)} %copy-done.4, f32[16,8,128]{2,1,0:T(8,128)S(1)} %copy-done.1, f32[16,8,128]{2,1,0:T(8,128)S(1)} %copy-done.2, f32[16,8,128]{2,1,0:T(8,128)S(1)} %copy-done.3, s32[7]{0:T(128)S(1)} %copy-done.5), custom_call_target="tpu_custom_call" | custom-call | tf_op jit(solution)/shard_map/schwarz/pallas_call | solution.py:468
  59.1 0.6 %copy.8 = f32[16,8,128]{2,1,0:T(8,128)} copy(f32[16,8,128]{2,1,0:T(8,128)S(1)} %schwarz.1) | data formatting | bytes 131072
Async XLA Ops:
  0.0 0.8 %copy-start = (s32[16,8,128]{2,1,0:T(8,128)S(1)}, s32[16,8,128]{2,1,0:T(8,128)}, u32[]{:S(2)}) copy-start(s32[16,8,128]{2,1,0:T(8,128)} %fac.1) | copy-start | bytes 196612
  0.8 0.8 %copy-start.1 = (f32[16,8,128]{2,1,0:T(8,128)S(1)}, f32[16,8,128]{2,1,0:T(8,128)}, u32[]{:S(2)}) copy-start(f32[16,8,128]{2,1,0:T(8,128)} %pscale.1) | copy-start | bytes 196612
  1.7 0.8 %copy-start.2 = (f32[16,8,128]{2,1,0:T(8,128)S(1)}, f32[16,8,128]{2,1,0:T(8,128)}, u32[]{:S(2)}) copy-start(f32[16,8,128]{2,1,0:T(8,128)} %src.1) | copy-start | bytes 196612
  2.5 0.8 %copy-start.3 = (f32[16,8,128]{2,1,0:T(8,128)S(1)}, f32[16,8,128]{2,1,0:T(8,128)}, u32[]{:S(2)}) copy-start(f32[16,8,128]{2,1,0:T(8,128)} %p0.1) | copy-start | bytes 196612
  3.4 0.7 %copy-start.4 = (f32[8]{0:T(128)S(1)}, f32[8]{0:T(128)}, u32[]{:S(2)}) copy-start(f32[8]{0:T(128)} %fperm.1) | copy-start | bytes 100
  4.0 0.7 %copy-start.5 = (s32[7]{0:T(128)S(1)}, s32[7]{0:T(128)}, u32[]{:S(2)}) copy-start(s32[7]{0:T(128)} %depth.1) | copy-start | bytes 88
where the time goes:
time: 60.4 us; the launch traced here: 59.7 us
  Pallas kernels  54.4 us (90%)
  local copies, waits for them, and re-layouts  5.3 us (9%)
    pallas_call x1, Pallas kernels, on_device(): pl.pallas_call(kernel, out_shape=jax.ShapeDtypeStruct(source.shape, f32),...  54.4 us
    unnamed x13, local copies, waits for them, and re-layouts  5.3 us

commit v1 on v0

--- a/solution.py
+++ b/solution.py
@@ -23,7 +23,9 @@
 CHUNKS = ROWS // BL
 CH = BL * 8
 
-DIRS = ((-1, 0), (1, 0), (0, -1), (0, 1), (-1, -1), (-1, 1), (1, -1), (1, 1))
+DIRS = (
+    (-1, 0), (1, 0), (0, -1), (0, 1), (-1, -1), (-1, 1), (1, -1), (1, 1), (0, -2), (0, 2)
+)
 OPP = tuple(DIRS.index((-a, -b)) for a, b in DIRS)
 
 
@@ -83,11 +85,13 @@
 
 
 def kernel(
-    fac, fperm, pscale, src, p0, depth, out,
+    fac_h, fperm_h, pscale_h, src_h, p0_h, depth_h, out,
+    fac, pscale, src, p0, fperm, depth, in_sem, gs, gr, c2r,
     zs, xs, ds, zr, xr, dr, mx, mzr, mxr, mdr, fzr, cs, cr,
     perm, pres, sper, spre, isrc, tgt, tside, e0, e1, e2, ub, corr,
     co, xf, yf, zf, gx, cx, sco, syf,
-    i_send, i_recv, m_send, m_recv, f_send, f_recv, c_send, c_recv,
+    i_send, i_recv, m_send, m_recv, f_send, f_recv, g_send, g_recv,
+    c_send, c_recv, c2_send, c2_recv,
 ):
     n_sub, n_grp = lax.axis_size("sub"), lax.axis_size("grp")
     sub, grp = lax.axis_index("sub"), lax.axis_index("grp")
@@ -96,6 +100,8 @@
         (1, 0): sub < n_sub - 1,
         (0, -1): grp > 0,
         (0, 1): grp < n_grp - 1,
+        (0, -2): grp > 1,
+        (0, 2): grp < n_grp - 2,
     }
     has = []
     for dz, dx in DIRS:
@@ -126,7 +132,23 @@
                 make(d, OPP[d]).wait_send()
                 make(d, d).wait_recv()
 
-    for d in range(8):
+    barrier = pltpu.get_barrier_semaphore()
+    for d in range(len(DIRS)):
+        @pl.when(has[d])
+        def _(d=d):
+            pl.semaphore_signal(barrier, inc=1, device_id=peer(d), device_id_type=MESH)
+
+    loads = [
+        pltpu.make_async_copy(a, b, in_sem.at[i])
+        for i, (a, b) in enumerate((
+            (fac_h, fac), (pscale_h, pscale), (p0_h, p0), (src_h, src),
+            (fperm_h, fperm), (depth_h, depth),
+        ))
+    ]
+    for load in loads:
+        load.start()
+
+    for d in range(len(DIRS)):
         @pl.when(jnp.logical_not(has[d]))
         def _(d=d):
             if d < 2:
@@ -136,17 +158,18 @@
             elif d < 4:
                 xr[d - 2] = jnp.zeros(xr.shape[1:], jnp.float32)
                 mxr[d - 2] = jnp.zeros(mxr.shape[1:], jnp.float32)
+                gr[d - 2] = jnp.zeros(gr.shape[1:], jnp.float32)
                 for ph in range(cr.shape[0]):
                     cr[ph, d - 2] = jnp.zeros(cr.shape[2:], jnp.float32)
-            else:
+            elif d < 8:
                 dr[d - 4] = jnp.zeros(dr.shape[1:], jnp.float32)
                 mdr[d - 4] = jnp.zeros(mdr.shape[1:], jnp.float32)
-
-    barrier = pltpu.get_barrier_semaphore()
-    for d in range(8):
-        @pl.when(has[d])
-        def _(d=d):
-            pl.semaphore_signal(barrier, inc=1, device_id=peer(d), device_id_type=MESH)
+            else:
+                for ph in range(c2r.shape[0]):
+                    c2r[ph, d - 8] = jnp.zeros(c2r.shape[2:], jnp.float32)
+
+    for load in loads:
+        load.wait()
 
     kinds = fac[...]
     own = jnp.zeros(kinds.shape, jnp.float32)
@@ -273,6 +296,19 @@
         edge, f = ub[here], xfac(here)
         for s in range(2):
             gx[s, here] = reduce_x(jnp.where(subl == 7 * s, edge, 0.0), f)
+        ub[here] = jnp.zeros((CH, LANES), jnp.float32)
+    for s in range(2):
+        near, far = (0, 1) if s == 0 else (7, 6)
+        for i in range(2):
+            gs[s, pl.ds(2 * i * ROWS, ROWS)] = gx[i, col(near)]
+            gs[s, pl.ds((2 * i + 1) * ROWS, ROWS)] = gx[i, col(far)]
+
+    def answer_copy(d, slot):
+        return remote(
+            d, gs.at[d - 2], gr.at[slot - 2], g_send.at[d - 2], g_recv.at[slot - 2]
+        )
+
+    exchange_start((2, 3), answer_copy)
 
     for s in range(2):
         mid = sper[s, 0, pl.ds(1, ROWS)]
@@ -302,17 +338,22 @@
         u = u + co[2, here] * roll_x(v, 1) + co[3, here] * roll_x(v, -1)
         return v, u + co[4, here] * roll_y(v, 1) + co[5, here] * roll_y(v, -1)
 
-    def col_copy(ph, rows):
+    def col_copy(ph):
         def make(d, slot):
+            if d < 4:
+                return remote(
+                    d, cs.at[ph, d - 2], cr.at[ph, slot - 2],
+                    c_send.at[ph, d - 2], c_recv.at[ph, slot - 2],
+                )
             return remote(
-                d, cs.at[ph, d - 2, pl.ds(0, rows)], cr.at[ph, slot - 2, pl.ds(0, rows)],
-                c_send.at[ph, d - 2], c_recv.at[ph, slot - 2],
+                d, cs.at[ph, d - 8, pl.ds(2 * ROWS, ROWS)], c2r.at[ph, slot - 8],
+                c2_send.at[ph, d - 8], c2_recv.at[ph, slot - 8],
             )
         return make
 
     def one_round(outer, k):
         first = isinstance(k, int)
-        ph = outer * 2 * ROUNDS + 2 * k
+        ph = outer * ROUNDS + k
         om = relax_weight(0)
         if not first:
             for i in range(1, ROUNDS):
@@ -324,68 +365,63 @@
             else:
                 v, u = update(tgt, e0, c)
                 e1[pl.ds((c * 8 + 1) * 8, CH)] = v + om * reduce_x(u, xfac(here))
-        if not first:
-            exchange_wait((2, 3), col_copy(ph, ROWS))
-            for z in range(ROWS):
-                at, here = pl.ds((z + 1) * 8, 8), pl.ds(z * 8, 8)
-                left = jnp.broadcast_to(cr[ph, 0, pl.ds(z, 1)], (8, LANES))
-                right = jnp.broadcast_to(cr[ph, 1, pl.ds(z, 1)], (8, LANES))
-                e1[at] = e1[at] + om * (gx[0, here] * left + gx[1, here] * right)
-        ph = ph + 1
         for s in range(2):
             near, far = (0, 1) if s == 0 else (7, 6)
             cs[ph, s, pl.ds(0, ROWS)] = e1[col(near, ROWS, 1)]
             cs[ph, s, pl.ds(ROWS, ROWS)] = e1[col(far, ROWS, 1)]
             if first:
                 cs[ph, s, pl.ds(2 * ROWS, ROWS)] = tgt[col(near)]
-        make = col_copy(ph, (3 if first else 2) * ROWS)
-        exchange_start((2, 3), make)
-        for c in range(CHUNKS):
-            here = pl.ds(c * CH, CH)
-            v, u = update(tgt, e1, c)
-            e2[pl.ds((c * 8 + 1) * 8, CH)] = v + om * reduce_y(u, [yf[i, here] for i in range(7)])
-        exchange_wait((2, 3), make)
-        beside = []
+            else:
+                cs[ph, s, pl.ds(2 * ROWS, ROWS)] = e0[col(near, ROWS, 1)]
+        dirs = (2, 3) if first else (2, 3, 8, 9)
+        exchange_start(dirs, col_copy(ph))
+        exchange_wait(dirs, col_copy(ph))
+        nears, fars = [], []
         for s in range(2):
             near, far = cr[ph, s, pl.ds(0, ROWS)], cr[ph, s, pl.ds(ROWS, ROWS)]
             if first:
                 tside[s] = cr[ph, s, pl.ds(2 * ROWS, ROWS)]
-            inner = e1[col(7 * s, ROWS, 1)]
+            else:
+                beyond, inner = c2r[ph, s], e0[col(7 * s, ROWS, 1)]
+                left, right = (beyond, inner) if s == 0 else (inner, beyond)
+                g = [gr[s, pl.ds(i * ROWS, ROWS)] for i in range(4)]
+                near = near + om * (g[0] * left + g[2] * right)
+                far = far + om * (g[1] * left + g[3] * right)
+            nears.append(near)
+            fars.append(far)
+            ub[col(7 * s)] = cx[s] * near
+        if not first:
+            for z in range(ROWS):
+                at, here = pl.ds((z + 1) * 8, 8), pl.ds(z * 8, 8)
+                left = jnp.broadcast_to(cr[ph, 0, pl.ds(2 * ROWS + z, 1)], (8, LANES))
+                right = jnp.broadcast_to(cr[ph, 1, pl.ds(2 * ROWS + z, 1)], (8, LANES))
+                e1[at] = e1[at] + om * (gx[0, here] * left + gx[1, here] * right)
+        for c in range(CHUNKS):
+            here = pl.ds(c * CH, CH)
+            v, u = update(tgt, e1, c)
+            u = u + ub[here]
+            e2[pl.ds((c * 8 + 1) * 8, CH)] = v + om * reduce_y(u, [yf[i, here] for i in range(7)])
+        for s in range(2):
+            near, far = nears[s], fars[s]
             u = tside[s] - near
             u = u + sco[s, 0] * roll_z(near, 1) + sco[s, 1] * roll_z(near, -1)
-            u = u + sco[s, 2] * far + sco[s, 3] * inner
+            u = u + sco[s, 2] * far + sco[s, 3] * e1[col(7 * s, ROWS, 1)]
             u = u + sco[s, 4] * roll_y(near, 1) + sco[s, 5] * roll_y(near, -1)
-            beside.append(near + om * reduce_y(u, [syf[s, i] for i in range(7)]))
-            f = [yf[i, col(7 * s)] for i in range(7)]
-            at = col(7 * s, ROWS, 1)
-            e2[at] = e2[at] + om * reduce_y(cx[s] * near, f)
+            beside = near + om * reduce_y(u, [syf[s, i] for i in range(7)])
+            ub[col(7 * s)] = cx[s] * beside
         for c in range(CHUNKS):
-            ub[pl.ds(c * CH, CH)] = update(tgt, e2, c)[1]
-        for s in range(2):
-            at = col(7 * s)
-            ub[at] = ub[at] + cx[s] * beside[s]
-        for c in range(CHUNKS):
+            v, u = update(tgt, e2, c)
+            u = u + ub[pl.ds(c * CH, CH)]
             fw, prev = [], None
             for i in range(BL):
-                at = pl.ds(c * CH + i * 8, 8)
-                prev = ub[at] if i == 0 else ub[at] - zf[0, at] * prev
+                at, r = pl.ds(c * CH + i * 8, 8), u[i * 8 : i * 8 + 8]
+                prev = r if i == 0 else r - zf[0, at] * prev
                 fw.append(prev)
             nxt = None
             for i in range(BL - 1, -1, -1):
                 at = pl.ds(c * CH + i * 8, 8)
                 nxt = fw[i] * zf[1, at] if nxt is None else fw[i] * zf[1, at] - zf[2, at] * nxt
-                to = pl.ds((c * 8 + i + 1) * 8, 8)
-                e0[to] = e2[to] + om * nxt
-
-        def send_next():
-            for s in range(2):
-                cs[ph + 1, s, pl.ds(0, ROWS)] = e0[col(7 * s, ROWS, 1)]
-            exchange_start((2, 3), col_copy(ph + 1, ROWS))
-
-        if first:
-            send_next()
-        else:
-            pl.when(k < ROUNDS - 1)(send_next)
+                e0[pl.ds((c * 8 + i + 1) * 8, 8)] = v[i * 8 : i * 8 + 8] + om * nxt
 
     def mid_copy(d, slot):
         if d < 2:
@@ -402,11 +438,14 @@
         return remote(d, a, fzr.at[slot], f_send.at[d], f_recv.at[slot])
 
     for outer in range(OUTER):
+        for s in range(2):
+            ub[col(7 * s)] = cx[s] * spre[s]
         for c in range(CHUNKS):
-            tgt[pl.ds(c * CH, CH)] = update(isrc, pres, c, active(rows_of(c)))[1]
-        for s in range(2):
-            tgt[col(7 * s)] = tgt[col(7 * s)] + cx[s] * spre[s]
+            u = update(isrc, pres, c, active(rows_of(c)))[1]
+            tgt[pl.ds(c * CH, CH)] = u + ub[pl.ds(c * CH, CH)]
         one_round(outer, 0)
+        if outer == 0:
+            exchange_wait((2, 3), answer_copy)
 
         def step(k, carry, outer=outer):
             one_round(outer, k)
@@ -450,8 +489,11 @@
         return pltpu.VMEM(shape, f32)
 
     field, wide = (ROWS * 8, LANES), (WIDE * 8, LANES)
-    phases = OUTER * 2 * ROUNDS
+    phases, own, dma = OUTER * ROUNDS, source.shape, pltpu.SemaphoreType.DMA
     scratch = [
+        pltpu.VMEM(own, jnp.int32), buf(*own), buf(*own), buf(*own),
+        pltpu.SMEM(facies_perm.shape, f32), pltpu.SMEM(intersection_depth.shape, jnp.int32),
+        dma((6,)), buf(2, 4 * ROWS, LANES), buf(2, 4 * ROWS, LANES), buf(phases, 2, ROWS, LANES),
         buf(2, 112, LANES), buf(2, 48, LANES), buf(4, 24, LANES),
         buf(2, 112, LANES), buf(2, 48, LANES), buf(4, 24, LANES),
         buf(2, ROWS, LANES), buf(2, 72, LANES), buf(2, ROWS, LANES), buf(4, 8, LANES),
@@ -462,17 +504,16 @@
         buf(6, *field), buf(4, *field), buf(7, *field), buf(3, *field),
         buf(2, *field), buf(2, ROWS, LANES), buf(2, 6, ROWS, LANES), buf(2, 7, ROWS, LANES),
     ]
-    sems = [pltpu.SemaphoreType.DMA((n,)) for n in (8, 8, 8, 8, 2, 2)]
-    sems += [pltpu.SemaphoreType.DMA((phases, 2)) for _ in range(2)]
-    vmem, smem = pl.BlockSpec(memory_space=pltpu.VMEM), pl.BlockSpec(memory_space=pltpu.SMEM)
+    sems = [dma((n,)) for n in (8, 8, 8, 8, 2, 2, 2, 2)]
+    sems += [dma((phases, 2)) for _ in range(4)]
     return pl.pallas_call(
         kernel,
         out_shape=jax.ShapeDtypeStruct(source.shape, f32),
-        in_specs=[vmem, smem, vmem, vmem, vmem, smem],
-        out_specs=vmem,
+        in_specs=[pl.BlockSpec(memory_space=pl.ANY)] * 6,
+        out_specs=pl.BlockSpec(memory_space=pltpu.VMEM),
         scratch_shapes=scratch + sems,
         compiler_params=pltpu.CompilerParams(
-            collective_id=0, has_side_effects=True, vmem_limit_bytes=32 * 1024 * 1024
+            collective_id=0, has_side_effects=True, vmem_limit_bytes=60 * 1024 * 1024
         ),
         name="schwarz",
     )(facies, facies_perm, perm_scale, source, pressure_start, intersection_depth)

time: 60.4 us -> 48.5 us (0.80)
  Pallas kernels: 54.4 us -> 46.8 us
  local copies, waits for them, and re-layouts: 5.3 us -> 1.47 us
    pallas_call x1, Pallas kernels: 54.4 us -> 46.8 us  [on_device(): pl.pallas_call(kernel, out_shape=jax.ShapeDtypeStruct(source.shape, f32),...]
    unnamed x13 -> x1, local copies, waits for them, and re-layouts: 5.3 us -> 1.47 us
where the time goes in v1:
time: 48.5 us; the launch traced here: 48.3 us
  Pallas kernels  46.8 us (96%)
  local copies, waits for them, and re-layouts  1.47 us (3%)
    pallas_call x1, Pallas kernels, on_device(): pl.pallas_call(kernel, out_shape=jax.ShapeDtypeStruct(source.shape, f32),...  46.8 us
    unnamed x1, local copies, waits for them, and re-layouts  1.47 us

profile of v1, /device:TPU:0, one launch (start us, length us, event | category | flops | bytes accessed | tf_op | source)
XLA Modules:
  0.0 48.3 jit_solution(5344750349120556893)
XLA Ops:
  0.0 46.8 %schwarz.1 = f32[16,8,128]{2,1,0:T(8,128)} custom-call(s32[16,8,128]{2,1,0:T(8,128)} %fac_h.1, f32[8]{0:T(128)} %fperm_h.1, f32[16,8,128]{2,1,0:T(8,128)} %pscale_h.1, f32[16,8,128]{2,1,0:T(8,128)} %src_h.1, f32[16,8,128]{2,1,0:T(8,128)} %p0_h.1, s32[7]{0:T(128)} %depth_h.1), custom_call_target="tpu_custom_call" | custom-call | tf_op jit(solution)/shard_map/schwarz/pallas_call | solution.py:509
  46.8 1.5 %copy.8 = f32[16,8,128]{2,1,0:T(8,128)} copy(f32[16,8,128]{2,1,0:T(8,128)} %schwarz.1) | data formatting | bytes 131072

commit v2 on v1

--- a/solution.py
+++ b/solution.py
@@ -86,12 +86,12 @@
 
 def kernel(
     fac_h, fperm_h, pscale_h, src_h, p0_h, depth_h, out,
-    fac, pscale, src, p0, fperm, depth, in_sem, gs, gr, c2r,
+    fac, pscale, src, p0, fperm, depth, in_sem, gs, gr, c2r, outs, outr, ycf,
     zs, xs, ds, zr, xr, dr, mx, mzr, mxr, mdr, fzr, cs, cr,
     perm, pres, sper, spre, isrc, tgt, tside, e0, e1, e2, ub, corr,
     co, xf, yf, zf, gx, cx, sco, syf,
     i_send, i_recv, m_send, m_recv, f_send, f_recv, g_send, g_recv,
-    c_send, c_recv, c2_send, c2_recv,
+    c_send, c_recv, c2_send, c2_recv, a_send, a_recv,
 ):
     n_sub, n_grp = lax.axis_size("sub"), lax.axis_size("grp")
     sub, grp = lax.axis_index("sub"), lax.axis_index("grp")
@@ -161,6 +161,7 @@
                 gr[d - 2] = jnp.zeros(gr.shape[1:], jnp.float32)
                 for ph in range(cr.shape[0]):
                     cr[ph, d - 2] = jnp.zeros(cr.shape[2:], jnp.float32)
+                    outr[ph, d - 2] = jnp.zeros(outr.shape[2:], jnp.float32)
             elif d < 8:
                 dr[d - 4] = jnp.zeros(dr.shape[1:], jnp.float32)
                 mdr[d - 4] = jnp.zeros(mdr.shape[1:], jnp.float32)
@@ -266,25 +267,6 @@
         a1, b1, a2, b2, a3, b3, iv = reduce_factors(fl, fr, roll_x)
         for i, f in enumerate((a2, b2, a3 + b3, iv)):
             xf[i, here] = f
-        fy = reduce_factors(
-            jnp.where(lane % BL == 0, 0.0, ff), jnp.where(lane % BL == BL - 1, 0.0, fk), roll_y
-        )
-        for i, f in enumerate(fy):
-            yf[i, here] = f
-        lz = -fb * active(rows_of(c) - 1)
-        uz = -fa * active(rows_of(c) + 1)
-        d = None
-        for i in range(BL):
-            at = pl.ds(c * CH + i * 8, 8)
-            part = slice(i * 8, i * 8 + 8)
-            if i == 0:
-                m, d = zeros_plane, jnp.ones((8, LANES), jnp.float32)
-            else:
-                m = lz[part] / d
-                d = 1.0 - m * uz[(i - 1) * 8 : i * 8]
-            zf[0, at] = m
-            zf[1, at] = 1.0 / d
-            zf[2, at] = uz[part] / d
     for s in range(2):
         cx[s] = ub[col(7 * s)]
 
@@ -292,43 +274,73 @@
         return [co[2, here], co[3, here]] + [xf[i, here] for i in range(4)]
 
     for c in range(CHUNKS):
-        here = pl.ds(c * CH, CH)
-        edge, f = ub[here], xfac(here)
-        for s in range(2):
-            gx[s, here] = reduce_x(jnp.where(subl == 7 * s, edge, 0.0), f)
-        ub[here] = jnp.zeros((CH, LANES), jnp.float32)
-    for s in range(2):
-        near, far = (0, 1) if s == 0 else (7, 6)
-        for i in range(2):
-            gs[s, pl.ds(2 * i * ROWS, ROWS)] = gx[i, col(near)]
-            gs[s, pl.ds((2 * i + 1) * ROWS, ROWS)] = gx[i, col(far)]
+        gx[0, pl.ds(c * CH, CH)] = ub[pl.ds(c * CH, CH)]
+        ub[pl.ds(c * CH, CH)] = jnp.zeros((CH, LANES), jnp.float32)
 
     def answer_copy(d, slot):
         return remote(
             d, gs.at[d - 2], gr.at[slot - 2], g_send.at[d - 2], g_recv.at[slot - 2]
         )
 
-    exchange_start((2, 3), answer_copy)
-
-    for s in range(2):
-        mid = sper[s, 0, pl.ds(1, ROWS)]
-        fb = harmonic(sper[s, 0, pl.ds(0, ROWS)], mid)
-        fa = harmonic(mid, sper[s, 0, pl.ds(2, ROWS)])
-        fx = harmonic(mid, sper[s, 1, pl.ds(1, ROWS)])
-        fo = harmonic(mid, perm[col(7 * s, ROWS, 1)])
-        ff = harmonic(jnp.where(lane2 == 0, 0.0, roll_y(mid, 1)), mid)
-        fk = harmonic(mid, jnp.where(lane2 == LANES - 1, 0.0, roll_y(mid, -1)))
-        inv = active(row2) / (STORE + fb + fa + fx + fo + ff + fk)
-        fb = jnp.where(row2 == 0, 0.0, fb * inv)
-        fa = jnp.where(row2 == ROWS - 1, 0.0, fa * inv)
-        ff, fk = ff * inv, fk * inv
-        for i, f in enumerate((fb, fa, fx * inv, fo * inv, ff, fk)):
-            sco[s, i] = f
-        fy = reduce_factors(
-            jnp.where(lane2 % BL == 0, 0.0, ff), jnp.where(lane2 % BL == BL - 1, 0.0, fk), roll_y
-        )
-        for i, f in enumerate(fy):
-            syf[s, i] = f
+    def rest_of_setup():
+        for c in range(CHUNKS):
+            here = pl.ds(c * CH, CH)
+            fb, fa, ff, fk = (co[i, here] for i in (0, 1, 4, 5))
+            fy = reduce_factors(
+                jnp.where(lane % BL == 0, 0.0, ff), jnp.where(lane % BL == BL - 1, 0.0, fk), roll_y
+            )
+            for i, f in enumerate(fy):
+                yf[i, here] = f
+            lz = -fb * active(rows_of(c) - 1)
+            uz = -fa * active(rows_of(c) + 1)
+            d = None
+            for i in range(BL):
+                at = pl.ds(c * CH + i * 8, 8)
+                part = slice(i * 8, i * 8 + 8)
+                if i == 0:
+                    m, d = zeros_plane, jnp.ones((8, LANES), jnp.float32)
+                else:
+                    m = lz[part] / d
+                    d = 1.0 - m * uz[(i - 1) * 8 : i * 8]
+                zf[0, at] = m
+                zf[1, at] = 1.0 / d
+                zf[2, at] = uz[part] / d
+        for c in range(CHUNKS):
+            here = pl.ds(c * CH, CH)
+            edge, f = gx[0, here], xfac(here)
+            for s in range(2):
+                gx[s, here] = reduce_x(jnp.where(subl == 7 * s, edge, 0.0), f)
+        for s in range(2):
+            near, far = (0, 1) if s == 0 else (7, 6)
+            for i in range(2):
+                gs[s, pl.ds(2 * i * ROWS, ROWS)] = gx[i, col(near)]
+                gs[s, pl.ds((2 * i + 1) * ROWS, ROWS)] = gx[i, col(far)]
+
+        exchange_start((2, 3), answer_copy)
+
+        for s in range(2):
+            for i in range(7):
+                ycf[s, i] = yf[i, col(7 * s)]
+
+        for s in range(2):
+            mid = sper[s, 0, pl.ds(1, ROWS)]
+            fb = harmonic(sper[s, 0, pl.ds(0, ROWS)], mid)
+            fa = harmonic(mid, sper[s, 0, pl.ds(2, ROWS)])
+            fx = harmonic(mid, sper[s, 1, pl.ds(1, ROWS)])
+            fo = harmonic(mid, perm[col(7 * s, ROWS, 1)])
+            ff = harmonic(jnp.where(lane2 == 0, 0.0, roll_y(mid, 1)), mid)
+            fk = harmonic(mid, jnp.where(lane2 == LANES - 1, 0.0, roll_y(mid, -1)))
+            inv = active(row2) / (STORE + fb + fa + fx + fo + ff + fk)
+            fb = jnp.where(row2 == 0, 0.0, fb * inv)
+            fa = jnp.where(row2 == ROWS - 1, 0.0, fa * inv)
+            ff, fk = ff * inv, fk * inv
+            for i, f in enumerate((fb, fa, fx * inv, fo * inv, ff, fk)):
+                sco[s, i] = f
+            fy = reduce_factors(
+                jnp.where(lane2 % BL == 0, 0.0, ff), jnp.where(lane2 % BL == BL - 1, 0.0, fk), roll_y
+            )
+            for i, f in enumerate(fy):
+                syf[s, i] = f
 
     def update(t, e, c, scale=None):
         here = pl.ds(c * CH, CH)
@@ -338,15 +350,23 @@
         u = u + co[2, here] * roll_x(v, 1) + co[3, here] * roll_x(v, -1)
         return v, u + co[4, here] * roll_y(v, 1) + co[5, here] * roll_y(v, -1)
 
-    def col_copy(ph):
+    def col_copy(ph, rows):
+        def make(d, slot):
+            return remote(
+                d, cs.at[ph, d - 2, pl.ds(0, rows)], cr.at[ph, slot - 2, pl.ds(0, rows)],
+                c_send.at[ph, d - 2], c_recv.at[ph, slot - 2],
+            )
+        return make
+
+    def solved_copy(ph):
         def make(d, slot):
             if d < 4:
                 return remote(
-                    d, cs.at[ph, d - 2], cr.at[ph, slot - 2],
-                    c_send.at[ph, d - 2], c_recv.at[ph, slot - 2],
+                    d, outs.at[ph, d - 2], outr.at[ph, slot - 2],
+                    a_send.at[ph, d - 2], a_recv.at[ph, slot - 2],
                 )
             return remote(
-                d, cs.at[ph, d - 8, pl.ds(2 * ROWS, ROWS)], c2r.at[ph, slot - 8],
+                d, outs.at[ph, d - 8], c2r.at[ph, slot - 8],
                 c2_send.at[ph, d - 8], c2_recv.at[ph, slot - 8],
             )
         return make
@@ -371,12 +391,22 @@
             cs[ph, s, pl.ds(ROWS, ROWS)] = e1[col(far, ROWS, 1)]
             if first:
                 cs[ph, s, pl.ds(2 * ROWS, ROWS)] = tgt[col(near)]
-            else:
-                cs[ph, s, pl.ds(2 * ROWS, ROWS)] = e0[col(near, ROWS, 1)]
-        dirs = (2, 3) if first else (2, 3, 8, 9)
-        exchange_start(dirs, col_copy(ph))
-        exchange_wait(dirs, col_copy(ph))
-        nears, fars = [], []
+        make = col_copy(ph, (3 if first else 2) * ROWS)
+        exchange_start((2, 3), make)
+        if first and outer == 0:
+            rest_of_setup()
+        if not first:
+            exchange_wait((2, 3, 8, 9), solved_copy(ph))
+            for z in range(ROWS):
+                at, here = pl.ds((z + 1) * 8, 8), pl.ds(z * 8, 8)
+                left = jnp.broadcast_to(outr[ph, 0, pl.ds(z, 1)], (8, LANES))
+                right = jnp.broadcast_to(outr[ph, 1, pl.ds(z, 1)], (8, LANES))
+                e1[at] = e1[at] + om * (gx[0, here] * left + gx[1, here] * right)
+        for c in range(CHUNKS):
+            here = pl.ds(c * CH, CH)
+            v, u = update(tgt, e1, c)
+            e2[pl.ds((c * 8 + 1) * 8, CH)] = v + om * reduce_y(u, [yf[i, here] for i in range(7)])
+        exchange_wait((2, 3), make)
         for s in range(2):
             near, far = cr[ph, s, pl.ds(0, ROWS)], cr[ph, s, pl.ds(ROWS, ROWS)]
             if first:
@@ -387,28 +417,14 @@
                 g = [gr[s, pl.ds(i * ROWS, ROWS)] for i in range(4)]
                 near = near + om * (g[0] * left + g[2] * right)
                 far = far + om * (g[1] * left + g[3] * right)
-            nears.append(near)
-            fars.append(far)
-            ub[col(7 * s)] = cx[s] * near
-        if not first:
-            for z in range(ROWS):
-                at, here = pl.ds((z + 1) * 8, 8), pl.ds(z * 8, 8)
-                left = jnp.broadcast_to(cr[ph, 0, pl.ds(2 * ROWS + z, 1)], (8, LANES))
-                right = jnp.broadcast_to(cr[ph, 1, pl.ds(2 * ROWS + z, 1)], (8, LANES))
-                e1[at] = e1[at] + om * (gx[0, here] * left + gx[1, here] * right)
-        for c in range(CHUNKS):
-            here = pl.ds(c * CH, CH)
-            v, u = update(tgt, e1, c)
-            u = u + ub[here]
-            e2[pl.ds((c * 8 + 1) * 8, CH)] = v + om * reduce_y(u, [yf[i, here] for i in range(7)])
-        for s in range(2):
-            near, far = nears[s], fars[s]
             u = tside[s] - near
             u = u + sco[s, 0] * roll_z(near, 1) + sco[s, 1] * roll_z(near, -1)
             u = u + sco[s, 2] * far + sco[s, 3] * e1[col(7 * s, ROWS, 1)]
             u = u + sco[s, 4] * roll_y(near, 1) + sco[s, 5] * roll_y(near, -1)
             beside = near + om * reduce_y(u, [syf[s, i] for i in range(7)])
             ub[col(7 * s)] = cx[s] * beside
+            at = col(7 * s, ROWS, 1)
+            e2[at] = e2[at] + om * reduce_y(cx[s] * near, [ycf[s, i] for i in range(7)])
         for c in range(CHUNKS):
             v, u = update(tgt, e2, c)
             u = u + ub[pl.ds(c * CH, CH)]
@@ -422,6 +438,16 @@
                 at = pl.ds(c * CH + i * 8, 8)
                 nxt = fw[i] * zf[1, at] if nxt is None else fw[i] * zf[1, at] - zf[2, at] * nxt
                 e0[pl.ds((c * 8 + i + 1) * 8, 8)] = v[i * 8 : i * 8 + 8] + om * nxt
+
+        def send_next():
+            for s in range(2):
+                outs[ph + 1, s] = e0[col(7 * s, ROWS, 1)]
+            exchange_start((2, 3, 8, 9), solved_copy(ph + 1))
+
+        if first:
+            send_next()
+        else:
+            pl.when(k < ROUNDS - 1)(send_next)
 
     def mid_copy(d, slot):
         if d < 2:
@@ -493,7 +519,8 @@
     scratch = [
         pltpu.VMEM(own, jnp.int32), buf(*own), buf(*own), buf(*own),
         pltpu.SMEM(facies_perm.shape, f32), pltpu.SMEM(intersection_depth.shape, jnp.int32),
-        dma((6,)), buf(2, 4 * ROWS, LANES), buf(2, 4 * ROWS, LANES), buf(phases, 2, ROWS, LANES),
+        dma((6,)), buf(2, 4 * ROWS, LANES), buf(2, 4 * ROWS, LANES),
+        *[buf(phases, 2, ROWS, LANES)] * 3, buf(2, 7, ROWS, LANES),
         buf(2, 112, LANES), buf(2, 48, LANES), buf(4, 24, LANES),
         buf(2, 112, LANES), buf(2, 48, LANES), buf(4, 24, LANES),
         buf(2, ROWS, LANES), buf(2, 72, LANES), buf(2, ROWS, LANES), buf(4, 8, LANES),
@@ -505,11 +532,11 @@
         buf(2, *field), buf(2, ROWS, LANES), buf(2, 6, ROWS, LANES), buf(2, 7, ROWS, LANES),
     ]
     sems = [dma((n,)) for n in (8, 8, 8, 8, 2, 2, 2, 2)]
-    sems += [dma((phases, 2)) for _ in range(4)]
+    sems += [dma((phases, 2)) for _ in range(6)]
     return pl.pallas_call(
         kernel,
         out_shape=jax.ShapeDtypeStruct(source.shape, f32),
-        in_specs=[pl.BlockSpec(memory_space=pl.ANY)] * 6,
+        in_specs=[pl.BlockSpec(memory_space=pltpu.HBM)] * 6,
         out_specs=pl.BlockSpec(memory_space=pltpu.VMEM),
         scratch_shapes=scratch + sems,
         compiler_params=pltpu.CompilerParams(

time: 48.5 us -> 47.2 us (0.973)
  Pallas kernels: 46.8 us -> 45.5 us
    pallas_call x1, Pallas kernels: 46.8 us -> 45.5 us  [on_device(): pl.pallas_call(kernel, out_shape=jax.ShapeDtypeStruct(source.shape, f32),...]
where the time goes in v2:
time: 47.2 us; the launch traced here: 47 us
  Pallas kernels  45.5 us (96%)
  local copies, waits for them, and re-layouts  1.47 us (3%)
    pallas_call x1, Pallas kernels, on_device(): pl.pallas_call(kernel, out_shape=jax.ShapeDtypeStruct(source.shape, f32),...  45.5 us
    unnamed x1, local copies, waits for them, and re-layouts  1.47 us

profile of v2, /device:TPU:0, one launch (start us, length us, event | category | flops | bytes accessed | tf_op | source)
XLA Modules:
  0.0 47.0 jit_solution(9100938579529190953)
XLA Ops:
  0.0 45.5 %schwarz.1 = f32[16,8,128]{2,1,0:T(8,128)} custom-call(s32[16,8,128]{2,1,0:T(8,128)} %fac_h.1, f32[8]{0:T(128)} %fperm_h.1, f32[16,8,128]{2,1,0:T(8,128)} %pscale_h.1, f32[16,8,128]{2,1,0:T(8,128)} %src_h.1, f32[16,8,128]{2,1,0:T(8,128)} %p0_h.1, s32[7]{0:T(128)} %depth_h.1), custom_call_target="tpu_custom_call" | custom-call | tf_op jit(solution)/shard_map/schwarz/pallas_call | solution.py:536
  45.6 1.5 %copy.8 = f32[16,8,128]{2,1,0:T(8,128)} copy(f32[16,8,128]{2,1,0:T(8,128)} %schwarz.1) | data formatting | bytes 131072

commit v3 on v2

--- a/solution.py
+++ b/solution.py
@@ -22,6 +22,7 @@
 LANES = 128
 CHUNKS = ROWS // BL
 CH = BL * 8
+PIECE = ROWS * 8
 
 DIRS = (
     (-1, 0), (1, 0), (0, -1), (0, 1), (-1, -1), (-1, 1), (1, -1), (1, 1), (0, -2), (0, 2)
@@ -342,11 +343,11 @@
             for i, f in enumerate(fy):
                 syf[s, i] = f
 
-    def update(t, e, c, scale=None):
-        here = pl.ds(c * CH, CH)
-        v = e[pl.ds((c * 8 + 1) * 8, CH)]
+    def update(t, e, at, scale=None):
+        here = pl.ds(at, PIECE)
+        v = e[pl.ds(at + 8, PIECE)]
         u = t[here] - (v if scale is None else v * scale)
-        u = u + co[0, here] * e[pl.ds(c * CH, CH)] + co[1, here] * e[pl.ds((c * 8 + 2) * 8, CH)]
+        u = u + co[0, here] * e[here] + co[1, here] * e[pl.ds(at + 16, PIECE)]
         u = u + co[2, here] * roll_x(v, 1) + co[3, here] * roll_x(v, -1)
         return v, u + co[4, here] * roll_y(v, 1) + co[5, here] * roll_y(v, -1)
 
@@ -378,13 +379,13 @@
         if not first:
             for i in range(1, ROUNDS):
                 om = jnp.where(k == i, jnp.float32(relax_weight(i)), om)
-        for c in range(CHUNKS):
-            here = pl.ds(c * CH, CH)
+        for at in range(0, ROWS * 8, PIECE):
+            here = pl.ds(at, PIECE)
             if first:
-                e1[pl.ds((c * 8 + 1) * 8, CH)] = om * reduce_x(tgt[here], xfac(here))
+                e1[pl.ds(at + 8, PIECE)] = om * reduce_x(tgt[here], xfac(here))
             else:
-                v, u = update(tgt, e0, c)
-                e1[pl.ds((c * 8 + 1) * 8, CH)] = v + om * reduce_x(u, xfac(here))
+                v, u = update(tgt, e0, at)
+                e1[pl.ds(at + 8, PIECE)] = v + om * reduce_x(u, xfac(here))
         for s in range(2):
             near, far = (0, 1) if s == 0 else (7, 6)
             cs[ph, s, pl.ds(0, ROWS)] = e1[col(near, ROWS, 1)]
@@ -402,10 +403,10 @@
                 left = jnp.broadcast_to(outr[ph, 0, pl.ds(z, 1)], (8, LANES))
                 right = jnp.broadcast_to(outr[ph, 1, pl.ds(z, 1)], (8, LANES))
                 e1[at] = e1[at] + om * (gx[0, here] * left + gx[1, here] * right)
-        for c in range(CHUNKS):
-            here = pl.ds(c * CH, CH)
-            v, u = update(tgt, e1, c)
-            e2[pl.ds((c * 8 + 1) * 8, CH)] = v + om * reduce_y(u, [yf[i, here] for i in range(7)])
+        for at in range(0, ROWS * 8, PIECE):
+            here = pl.ds(at, PIECE)
+            v, u = update(tgt, e1, at)
+            e2[pl.ds(at + 8, PIECE)] = v + om * reduce_y(u, [yf[i, here] for i in range(7)])
         exchange_wait((2, 3), make)
         for s in range(2):
             near, far = cr[ph, s, pl.ds(0, ROWS)], cr[ph, s, pl.ds(ROWS, ROWS)]
@@ -425,19 +426,21 @@
             ub[col(7 * s)] = cx[s] * beside
             at = col(7 * s, ROWS, 1)
             e2[at] = e2[at] + om * reduce_y(cx[s] * near, [ycf[s, i] for i in range(7)])
-        for c in range(CHUNKS):
-            v, u = update(tgt, e2, c)
-            u = u + ub[pl.ds(c * CH, CH)]
-            fw, prev = [], None
-            for i in range(BL):
-                at, r = pl.ds(c * CH + i * 8, 8), u[i * 8 : i * 8 + 8]
-                prev = r if i == 0 else r - zf[0, at] * prev
-                fw.append(prev)
+        for at in range(0, ROWS * 8, PIECE):
+            v, u = update(tgt, e2, at)
+            u = (u + ub[pl.ds(at, PIECE)]).reshape(PIECE // CH, BL, 8, LANES)
+            m, iv, up = (zf[i, pl.ds(at, PIECE)].reshape(u.shape) for i in range(3))
+            v = v.reshape(u.shape)
+            fw = [u[:, 0]]
+            for i in range(1, BL):
+                fw.append(u[:, i] - m[:, i] * fw[-1])
             nxt = None
             for i in range(BL - 1, -1, -1):
-                at = pl.ds(c * CH + i * 8, 8)
-                nxt = fw[i] * zf[1, at] if nxt is None else fw[i] * zf[1, at] - zf[2, at] * nxt
-                e0[pl.ds((c * 8 + i + 1) * 8, 8)] = v[i * 8 : i * 8 + 8] + om * nxt
+                x = fw[i] * iv[:, i]
+                nxt = x if nxt is None else x - up[:, i] * nxt
+                new = v[:, i] + om * nxt
+                for c in range(PIECE // CH):
+                    e0[pl.ds(at + c * CH + (i + 1) * 8, 8)] = new[c]
 
         def send_next():
             for s in range(2):
@@ -466,9 +469,10 @@
     for outer in range(OUTER):
         for s in range(2):
             ub[col(7 * s)] = cx[s] * spre[s]
-        for c in range(CHUNKS):
-            u = update(isrc, pres, c, active(rows_of(c)))[1]
-            tgt[pl.ds(c * CH, CH)] = u + ub[pl.ds(c * CH, CH)]
+        for c in range(0, CHUNKS, PIECE // CH):
+            rows = [active(rows_of(i)) for i in range(c, c + PIECE // CH)]
+            here = pl.ds(c * CH, PIECE)
+            tgt[here] = update(isrc, pres, c * CH, jnp.concatenate(rows))[1] + ub[here]
         one_round(outer, 0)
         if outer == 0:
             exchange_wait((2, 3), answer_copy)

time: 47.2 us -> 47.4 us (level)
  no operation moved by 1% of the time
where the time goes in v3:
time: 47.4 us; the launch traced here: 47.2 us
  Pallas kernels  45.7 us (96%)
  local copies, waits for them, and re-layouts  1.47 us (3%)
    pallas_call x1, Pallas kernels, on_device(): pl.pallas_call(kernel, out_shape=jax.ShapeDtypeStruct(source.shape, f32),...  45.7 us
    unnamed x1, local copies, waits for them, and re-layouts  1.47 us

profile of v3, /device:TPU:0, one launch (start us, length us, event | category | flops | bytes accessed | tf_op | source)
XLA Modules:
  0.0 47.2 jit_solution(4372600895435029364)
XLA Ops:
  0.0 45.7 %schwarz.1 = f32[16,8,128]{2,1,0:T(8,128)} custom-call(s32[16,8,128]{2,1,0:T(8,128)} %fac_h.1, f32[8]{0:T(128)} %fperm_h.1, f32[16,8,128]{2,1,0:T(8,128)} %pscale_h.1, f32[16,8,128]{2,1,0:T(8,128)} %src_h.1, f32[16,8,128]{2,1,0:T(8,128)} %p0_h.1, s32[7]{0:T(128)} %depth_h.1), custom_call_target="tpu_custom_call" | custom-call | tf_op jit(solution)/shard_map/schwarz/pallas_call | solution.py:540
  45.7 1.5 %copy.8 = f32[16,8,128]{2,1,0:T(8,128)} copy(f32[16,8,128]{2,1,0:T(8,128)} %schwarz.1) | data formatting | bytes 131072

commit v4 on v3

--- a/solution.py
+++ b/solution.py
@@ -22,7 +22,7 @@
 LANES = 128
 CHUNKS = ROWS // BL
 CH = BL * 8
-PIECE = ROWS * 8
+PIECE = CH
 
 DIRS = (
     (-1, 0), (1, 0), (0, -1), (0, 1), (-1, -1), (-1, 1), (1, -1), (1, 1), (0, -2), (0, 2)
@@ -130,8 +130,14 @@
         for d in dirs:
             @pl.when(has[d])
             def _(d=d):
-                make(d, OPP[d]).wait_send()
                 make(d, d).wait_recv()
+
+    def exchange_sent(dirs, makes):
+        for d in dirs:
+            @pl.when(has[d])
+            def _(d=d):
+                for make in makes:
+                    make(d, OPP[d]).wait_send()
 
     barrier = pltpu.get_barrier_semaphore()
     for d in range(len(DIRS)):
@@ -170,44 +176,48 @@
                 for ph in range(c2r.shape[0]):
                     c2r[ph, d - 8] = jnp.zeros(c2r.shape[2:], jnp.float32)
 
-    for load in loads:
-        load.wait()
-
+    for i in (0, 1, 4):
+        loads[i].wait()
     kinds = fac[...]
     own = jnp.zeros(kinds.shape, jnp.float32)
     for kind in range(FACIES):
         own = jnp.where(kinds == kind, fperm[kind], own)
-    own = (own * pscale[...]).reshape(OWN * 8, LANES)
-    perm[pl.ds(40, OWN * 8)] = own
-    pres[pl.ds(40, OWN * 8)] = p0[...].reshape(OWN * 8, LANES)
-    isrc[pl.ds(32, OWN * 8)] = src[...].reshape(OWN * 8, LANES)
+    perm[pl.ds(40, OWN * 8)] = (own * pscale[...]).reshape(OWN * 8, LANES)
     for s in range(2):
-        at = 5 if s == 0 else 16
-        zs[s, pl.ds(0, 40)] = perm[pl.ds(at * 8, 40)]
-        zs[s, pl.ds(40, 40)] = pres[pl.ds(at * 8, 40)]
-        zs[s, pl.ds(80, 32)] = isrc[pl.ds(32 if s == 0 else 128, 32)]
         near, far = (0, 1) if s == 0 else (7, 6)
-        kn, kf, pn = perm[col(near, 16, 5)], perm[col(far, 16, 5)], pres[col(near, 16, 5)]
-        xs[s, pl.ds(0, 16)] = kn
-        xs[s, pl.ds(16, 16)] = kf
-        xs[s, pl.ds(32, 16)] = pn
+        zs[s, pl.ds(0, 40)] = perm[pl.ds(40 if s == 0 else 128, 40)]
+        xs[s, pl.ds(0, 16)] = perm[col(near, 16, 5)]
+        xs[s, pl.ds(16, 16)] = perm[col(far, 16, 5)]
         for z in range(2):
             at_rows = 5 if z == 0 else 13
             ds[2 * z + s, pl.ds(0, 8)] = perm[col(near, 8, at_rows)]
             ds[2 * z + s, pl.ds(8, 8)] = perm[col(far, 8, at_rows)]
-            ds[2 * z + s, pl.ds(16, 8)] = pres[col(near, 8, at_rows)]
-
-    def init_copy(d, slot):
-        if d < 2:
-            a, b = zs.at[d], zr.at[slot]
-        elif d < 4:
-            a, b = xs.at[d - 2], xr.at[slot - 2]
-        else:
-            a, b = ds.at[d - 4], dr.at[slot - 4]
-        return remote(d, a, b, i_send.at[d], i_recv.at[slot])
+
+    def init_copy(part):
+        def make(d, slot):
+            if d < 2:
+                at, a, b = (pl.ds(0, 40), pl.ds(40, 72))[part], zs.at[d], zr.at[slot]
+            elif d < 4:
+                at, a, b = (pl.ds(0, 32), pl.ds(32, 16))[part], xs.at[d - 2], xr.at[slot - 2]
+            else:
+                at, a, b = (pl.ds(0, 16), pl.ds(16, 8))[part], ds.at[d - 4], dr.at[slot - 4]
+            return remote(d, a.at[at], b.at[at], i_send.at[part, d], i_recv.at[part, slot])
+        return make
 
     pl.semaphore_wait(barrier, sum(jnp.where(h, 1, 0) for h in has))
-    exchange_start(range(8), init_copy)
+    exchange_start(range(8), init_copy(0))
+    for i in (2, 3, 5):
+        loads[i].wait()
+    pres[pl.ds(40, OWN * 8)] = p0[...].reshape(OWN * 8, LANES)
+    isrc[pl.ds(32, OWN * 8)] = src[...].reshape(OWN * 8, LANES)
+    for s in range(2):
+        near = 7 * s
+        zs[s, pl.ds(40, 40)] = pres[pl.ds(40 if s == 0 else 128, 40)]
+        zs[s, pl.ds(80, 32)] = isrc[pl.ds(32 if s == 0 else 128, 32)]
+        xs[s, pl.ds(32, 16)] = pres[col(near, 16, 5)]
+        for z in range(2):
+            ds[2 * z + s, pl.ds(16, 8)] = pres[col(near, 8, 5 if z == 0 else 13)]
+    exchange_start(range(8), init_copy(1))
 
     low = jnp.where(sub > 0, depth[jnp.maximum(sub - 1, 0)], 0)
     high = jnp.where(sub < n_sub - 1, depth[jnp.minimum(sub, n_sub - 2)], 0)
@@ -228,22 +238,14 @@
         e[pl.ds(0, 8)] = zeros_plane
         e[pl.ds((ROWS + 1) * 8, 8)] = zeros_plane
 
-    exchange_wait(range(8), init_copy)
-
+    exchange_wait(range(8), init_copy(0))
     perm[pl.ds(0, 40)] = zr[0, pl.ds(0, 40)]
-    pres[pl.ds(0, 40)] = zr[0, pl.ds(40, 40)]
-    isrc[pl.ds(0, 32)] = zr[0, pl.ds(80, 32)]
     perm[pl.ds(168, 40)] = zr[1, pl.ds(0, 40)]
-    pres[pl.ds(168, 40)] = zr[1, pl.ds(40, 40)]
-    isrc[pl.ds(160, 32)] = zr[1, pl.ds(80, 32)]
     for s in range(2):
         for f in range(2):
             sper[s, f, pl.ds(5, 16)] = xr[s, pl.ds(16 * f, 16)]
             sper[s, f, pl.ds(0, 5)] = dr[s, pl.ds(8 * f + 3, 5)]
             sper[s, f, pl.ds(21, 5)] = dr[2 + s, pl.ds(8 * f, 5)]
-        spre[s, pl.ds(4, 16)] = xr[s, pl.ds(32, 16)]
-        spre[s, pl.ds(0, 4)] = dr[s, pl.ds(20, 4)]
-        spre[s, pl.ds(20, 4)] = dr[2 + s, pl.ds(16, 4)]
         ub[col(7 * s)] = sper[s, 0, pl.ds(1, ROWS)]
 
     for c in range(CHUNKS):
@@ -264,7 +266,7 @@
         fb, fa, ff, fk = fb * inv, fa * inv, ff * inv, fk * inv
         for i, f in enumerate((fb, fa, fl, fr, ff, fk)):
             co[i, here] = f
-        isrc[here] = isrc[here] * inv
+        zf[0, here] = inv
         a1, b1, a2, b2, a3, b3, iv = reduce_factors(fl, fr, roll_x)
         for i, f in enumerate((a2, b2, a3 + b3, iv)):
             xf[i, here] = f
@@ -274,6 +276,16 @@
     def xfac(here):
         return [co[2, here], co[3, here]] + [xf[i, here] for i in range(4)]
 
+    exchange_wait(range(8), init_copy(1))
+    pres[pl.ds(0, 40)] = zr[0, pl.ds(40, 40)]
+    isrc[pl.ds(0, 32)] = zr[0, pl.ds(80, 32)]
+    pres[pl.ds(168, 40)] = zr[1, pl.ds(40, 40)]
+    isrc[pl.ds(160, 32)] = zr[1, pl.ds(80, 32)]
+    isrc[...] = isrc[...] * zf[0]
+    for s in range(2):
+        spre[s, pl.ds(4, 16)] = xr[s, pl.ds(32, 16)]
+        spre[s, pl.ds(0, 4)] = dr[s, pl.ds(20, 4)]
+        spre[s, pl.ds(20, 4)] = dr[2 + s, pl.ds(16, 4)]
     for c in range(CHUNKS):
         gx[0, pl.ds(c * CH, CH)] = ub[pl.ds(c * CH, CH)]
         ub[pl.ds(c * CH, CH)] = jnp.zeros((CH, LANES), jnp.float32)
@@ -482,6 +494,8 @@
             return carry
 
         lax.fori_loop(1, ROUNDS, step, 0)
+        if outer == 1:
+            exchange_sent(range(8), [mid_copy])
         for c in range(CHUNKS):
             rows = rows_of(c)
             band = (rows < OV + low) | (rows >= OV + OWN - high)
@@ -503,6 +517,13 @@
                     spre[s, at] = spre[s, at] + mdr[2 * z + s]
         else:
             exchange_start((0, 1), end_copy)
+            later = [k for k in range(OUTER * ROUNDS) if k % ROUNDS]
+            exchange_sent(range(8), [init_copy(0), init_copy(1)])
+            makes = [col_copy(k, (2 if k % ROUNDS else 3) * ROWS) for k in range(OUTER * ROUNDS)]
+            makes += [solved_copy(k) for k in later]
+            exchange_sent((2, 3), makes + [answer_copy])
+            exchange_sent((8, 9), [solved_copy(k) for k in later])
+            exchange_sent((0, 1), [end_copy])
             pres[pl.ds(8, ROWS * 8)] = pres[pl.ds(8, ROWS * 8)] + corr[...]
             exchange_wait((0, 1), end_copy)
             for z in range(2):
@@ -535,7 +556,7 @@
         buf(6, *field), buf(4, *field), buf(7, *field), buf(3, *field),
         buf(2, *field), buf(2, ROWS, LANES), buf(2, 6, ROWS, LANES), buf(2, 7, ROWS, LANES),
     ]
-    sems = [dma((n,)) for n in (8, 8, 8, 8, 2, 2, 2, 2)]
+    sems = [dma((2, 8)), dma((2, 8))] + [dma((n,)) for n in (8, 8, 2, 2, 2, 2)]
     sems += [dma((phases, 2)) for _ in range(6)]
     return pl.pallas_call(
         kernel,

time: 47.4 us -> 47 us (level)
  no operation moved by 1% of the time
where the time goes in v4:
time: 47 us; the launch traced here: 46.8 us
  Pallas kernels  45.3 us (96%)
  local copies, waits for them, and re-layouts  1.47 us (3%)
    pallas_call x1, Pallas kernels, on_device(): pl.pallas_call(kernel, out_shape=jax.ShapeDtypeStruct(source.shape, f32),...  45.3 us
    unnamed x1, local copies, waits for them, and re-layouts  1.47 us

profile of v4, /device:TPU:0, one launch (start us, length us, event | category | flops | bytes accessed | tf_op | source)
XLA Modules:
  0.0 46.8 jit_solution(7719365945459972232)
XLA Ops:
  0.0 45.3 %schwarz.1 = f32[16,8,128]{2,1,0:T(8,128)} custom-call(s32[16,8,128]{2,1,0:T(8,128)} %fac_h.1, f32[8]{0:T(128)} %fperm_h.1, f32[16,8,128]{2,1,0:T(8,128)} %pscale_h.1, f32[16,8,128]{2,1,0:T(8,128)} %src_h.1, f32[16,8,128]{2,1,0:T(8,128)} %p0_h.1, s32[7]{0:T(128)} %depth_h.1), custom_call_target="tpu_custom_call" | custom-call | tf_op jit(solution)/shard_map/schwarz/pallas_call | solution.py:561
  45.3 1.5 %copy.8 = f32[16,8,128]{2,1,0:T(8,128)} copy(f32[16,8,128]{2,1,0:T(8,128)} %schwarz.1) | data formatting | bytes 131072

commit v5 on v4

--- a/solution.py
+++ b/solution.py
@@ -406,8 +406,8 @@
                 cs[ph, s, pl.ds(2 * ROWS, ROWS)] = tgt[col(near)]
         make = col_copy(ph, (3 if first else 2) * ROWS)
         exchange_start((2, 3), make)
-        if first and outer == 0:
-            rest_of_setup()
+        if first:
+            pl.when(outer == 0)(rest_of_setup)
         if not first:
             exchange_wait((2, 3, 8, 9), solved_copy(ph))
             for z in range(ROWS):
@@ -478,7 +478,7 @@
         a = corr.at[pl.ds(0 if d == 0 else 160, 32)]
         return remote(d, a, fzr.at[slot], f_send.at[d], f_recv.at[slot])
 
-    for outer in range(OUTER):
+    def iteration(outer, carry):
         for s in range(2):
             ub[col(7 * s)] = cx[s] * spre[s]
         for c in range(0, CHUNKS, PIECE // CH):
@@ -486,22 +486,29 @@
             here = pl.ds(c * CH, PIECE)
             tgt[here] = update(isrc, pres, c * CH, jnp.concatenate(rows))[1] + ub[here]
         one_round(outer, 0)
-        if outer == 0:
+
+        @pl.when(outer == 0)
+        def _():
             exchange_wait((2, 3), answer_copy)
 
-        def step(k, carry, outer=outer):
+        def step(k, carry):
             one_round(outer, k)
             return carry
 
         lax.fori_loop(1, ROUNDS, step, 0)
-        if outer == 1:
+
+        @pl.when(outer == 1)
+        def _():
             exchange_sent(range(8), [mid_copy])
+
         for c in range(CHUNKS):
             rows = rows_of(c)
             band = (rows < OV + low) | (rows >= OV + OWN - high)
             w = active(rows) * jnp.where(band, 0.5, 1.0)
             corr[pl.ds(c * CH, CH)] = w * e0[pl.ds((c * 8 + 1) * 8, CH)]
-        if outer == 0:
+
+        @pl.when(outer == 0)
+        def _():
             for s in range(2):
                 mx[s] = corr[col(7 * s)]
             exchange_start(range(8), mid_copy)
@@ -515,7 +522,9 @@
                 for z in range(2):
                     at = pl.ds(16 * z, 8)
                     spre[s, at] = spre[s, at] + mdr[2 * z + s]
-        else:
+
+        @pl.when(outer == 1)
+        def _():
             exchange_start((0, 1), end_copy)
             later = [k for k in range(OUTER * ROUNDS) if k % ROUNDS]
             exchange_sent(range(8), [init_copy(0), init_copy(1)])
@@ -529,6 +538,9 @@
             for z in range(2):
                 at = pl.ds(40 if z == 0 else 17 * 8, 32)
                 pres[at] = pres[at] + fzr[z]
+        return carry
+
+    lax.fori_loop(0, OUTER, iteration, 0)
     out[...] = pres[pl.ds(40, OWN * 8)].reshape(OWN, 8, LANES)
 
 

time: 47 us -> 47.1 us (level)
  no operation moved by 1% of the time
where the time goes in v5:
time: 47.1 us; the launch traced here: 46.9 us
  Pallas kernels  45.4 us (96%)
  local copies, waits for them, and re-layouts  1.47 us (3%)
    pallas_call x1, Pallas kernels, on_device(): pl.pallas_call(kernel, out_shape=jax.ShapeDtypeStruct(source.shape, f32),...  45.4 us
    unnamed x1, local copies, waits for them, and re-layouts  1.47 us

profile of v5, /device:TPU:0, one launch (start us, length us, event | category | flops | bytes accessed | tf_op | source)
XLA Modules:
  0.0 46.9 jit_solution(15711764582828369651)
XLA Ops:
  0.0 45.4 %schwarz.1 = f32[16,8,128]{2,1,0:T(8,128)} custom-call(s32[16,8,128]{2,1,0:T(8,128)} %fac_h.1, f32[8]{0:T(128)} %fperm_h.1, f32[16,8,128]{2,1,0:T(8,128)} %pscale_h.1, f32[16,8,128]{2,1,0:T(8,128)} %src_h.1, f32[16,8,128]{2,1,0:T(8,128)} %p0_h.1, s32[7]{0:T(128)} %depth_h.1), custom_call_target="tpu_custom_call" | custom-call | tf_op jit(solution)/shard_map/schwarz/pallas_call | solution.py:573
  45.4 1.5 %copy.8 = f32[16,8,128]{2,1,0:T(8,128)} copy(f32[16,8,128]{2,1,0:T(8,128)} %schwarz.1) | data formatting | bytes 131072

commit v6 on v4

--- a/solution.py
+++ b/solution.py
@@ -409,7 +409,7 @@
         if first and outer == 0:
             rest_of_setup()
         if not first:
-            exchange_wait((2, 3, 8, 9), solved_copy(ph))
+            exchange_wait((2, 3), solved_copy(ph))
             for z in range(ROWS):
                 at, here = pl.ds((z + 1) * 8, 8), pl.ds(z * 8, 8)
                 left = jnp.broadcast_to(outr[ph, 0, pl.ds(z, 1)], (8, LANES))
@@ -420,6 +420,8 @@
             v, u = update(tgt, e1, at)
             e2[pl.ds(at + 8, PIECE)] = v + om * reduce_y(u, [yf[i, here] for i in range(7)])
         exchange_wait((2, 3), make)
+        if not first:
+            exchange_wait((8, 9), solved_copy(ph))
         for s in range(2):
             near, far = cr[ph, s, pl.ds(0, ROWS)], cr[ph, s, pl.ds(ROWS, ROWS)]
             if first:

time: 47 us -> 45 us (0.957)
  Pallas kernels: 45.3 us -> 43.3 us
    pallas_call x1, Pallas kernels: 45.3 us -> 43.3 us  [on_device(): pl.pallas_call(kernel, out_shape=jax.ShapeDtypeStruct(source.shape, f32),...]
where the time goes in v6:
time: 45 us; the launch traced here: 44.8 us
  Pallas kernels  43.3 us (96%)
  local copies, waits for them, and re-layouts  1.47 us (3%)
    pallas_call x1, Pallas kernels, on_device(): pl.pallas_call(kernel, out_shape=jax.ShapeDtypeStruct(source.shape, f32),...  43.3 us
    unnamed x1, local copies, waits for them, and re-layouts  1.47 us

profile of v6, /device:TPU:0, one launch (start us, length us, event | category | flops | bytes accessed | tf_op | source)
XLA Modules:
  0.0 44.8 jit_solution(15240037236680951788)
XLA Ops:
  0.0 43.3 %schwarz.1 = f32[16,8,128]{2,1,0:T(8,128)} custom-call(s32[16,8,128]{2,1,0:T(8,128)} %fac_h.1, f32[8]{0:T(128)} %fperm_h.1, f32[16,8,128]{2,1,0:T(8,128)} %pscale_h.1, f32[16,8,128]{2,1,0:T(8,128)} %src_h.1, f32[16,8,128]{2,1,0:T(8,128)} %p0_h.1, s32[7]{0:T(128)} %depth_h.1), custom_call_target="tpu_custom_call" | custom-call | tf_op jit(solution)/shard_map/schwarz/pallas_call | solution.py:563
  43.3 1.5 %copy.8 = f32[16,8,128]{2,1,0:T(8,128)} copy(f32[16,8,128]{2,1,0:T(8,128)} %schwarz.1) | data formatting | bytes 131072
